TPU v7x, 256 devices: a whole 4x4x8 slice. The times are simulated.
256 devices in a mesh: wide: 32 (over x, z_lo, y), narrow: 8 (over z_hi, core).
Axes of the slice: x: 4, y: 4, z: 8 (z_hi: 4, z_lo: 2; z = z_hi * 2 + z_lo), core: 2. Of those that a mesh axis runs over, the one named last changes fastest.
Arguments:
- amplitudes: float32 [2048, 24576], P('narrow', 'wide'), may hold values from -6 to 6
- integrals: float32 [24576, 2, 8192], P('wide', None, 'narrow'), may hold values from -0.109375 to 0.109375
- ab_sizes: int32 [8], replicated, may hold values from 1 to 6144, 24576 in all
- cd_sizes: int32 [2, 8], replicated, may hold values from 1 to 2048, 8192 in all within a row
Outputs:
- ladder: float32 [2048, 2, 8192], P('wide', None, 'narrow')
Inputs may be any that keep to these rules, and one draw needn't show every extreme that they name: `ab_sizes`: each entry is at least 1 and the entries sum to 24576; the largest is exactly 6144. `cd_sizes`: each row's entries are at least 1 and sum to 8192; the largest of each row is exactly 2048.
All inputs are finite; a program needn't handle non-finite values.
Results may differ from a plain program's by a relative error of at most 0.0003.
Values sent between devices are 32-bit elements; how exact they have to be, the bound alone decides.
A program may use at most 128 MiB of HBM per device.

v0:
```python
import jax
import jax.numpy as jnp
from jax import lax
from jax.sharding import PartitionSpec as P


def irrep_labels(positions, sizes):
    block_ends = jnp.cumsum(sizes, axis=-1)
    return jnp.sum((positions[..., None] >= block_ends).astype(jnp.int32), axis=-1)


def shards(amplitudes, integrals, ab_sizes, cd_sizes):
    pair_rows = integrals.shape[0]
    slab_count = integrals.shape[1]
    slab_cols = integrals.shape[2]
    ab_positions = lax.axis_index("wide") * pair_rows + lax.iota(jnp.int32, pair_rows)
    cd_positions = lax.axis_index("narrow") * slab_cols + lax.iota(jnp.int32, slab_cols)
    ab_label = irrep_labels(ab_positions, ab_sizes)
    cd_label = irrep_labels(cd_positions[None, :], cd_sizes[:, None, :])
    masked = jnp.where(
        ab_label[:, None, None] == cd_label[None, :, :], integrals, jnp.zeros((), integrals.dtype)
    )
    gathered = lax.all_gather(amplitudes, "narrow", axis=0, tiled=True)
    results = []
    for slab_index in range(slab_count):
        slab_tile = masked[:, slab_index, :]
        results.append(
            lax.psum_scatter(
                jnp.dot(
                    gathered,
                    slab_tile,
                    precision=lax.Precision.HIGHEST,
                    preferred_element_type=jnp.float32,
                ),
                "wide",
                scatter_dimension=0,
                tiled=True,
            )
        )
    return jnp.stack(results, axis=1)


def solution(mesh):
    return jax.shard_map(
        shards,
        mesh=mesh,
        in_specs=(P("narrow", "wide"), P("wide", None, "narrow"), P(), P()),
        out_specs=P("wide", None, "narrow"),
        check_vma=False,
    )
```

profile of v0, /device:TPU:64, one launch (start us, length us, event | category | flops | bytes accessed | tf_op | source)
XLA Modules:
  0.0 506.0 jit_solution(9498958789586117649)
XLA Ops:
  6.5 0.0 all-gather.2.cloned.1.call-start
  6.5 0.7 all-gather.2.cloned.1.call-update
  7.3 0.0 reduce-scatter.7.cloned.1.call-start
  7.3 0.8 reduce-window.8
  8.1 0.9 reduce_window_sum.18
  9.0 0.1 convert_reduce_fusion.1
  9.1 0.1 convert_reduce_fusion
  9.2 7.9 %copy_select_fusion = f32[768,2,1024]{2,0,1:T(8,128)} fusion(f32[768,2,1024]{2,1,0:T(2,128)} %param.5, s32[2,1024]{1,0:T(2,128)S(1)} %convert_reduce_fusion, s32[768]{0:T(1024)S(1)} %convert_reduce_fusion.1), kind=kLoop, calls=%fused_computation | loop fusion | flops 3145728 | bytes 12594176 | tf_op jit(solution)/shard_map/jit(_where)/select_n | solution.py:20
  17.0 64.5 %all-gather.2.cloned.1.call-done = f32[2048,768]{1,0:T(8,128)} async-done(((f32[256,768]{1,0:T(8,128)}), f32[2048,768]{1,0:T(8,128)}) %all-gather.2.cloned.1.call-update) | async-done | bytes 6291472 | tf_op jit(solution)/shard_map/all_gather | solution.py:23
  81.6 44.4 %convolution_bitcast_fusion.1 = f32[2048,1024]{0,1:T(8,128)} fusion(f32[2048,768]{1,0:T(8,128)} %all-gather.2.cloned.1.call-done, f32[768,2,1024]{2,0,1:T(8,128)} %copy_select_fusion), kind=kOutput, calls=%fused_computation.2 | convolution fusion | flops 19327352832 | bytes 17825792 | tf_op jit(solution)/shard_map/dot_general | solution.py:29
  126.0 9.3 %copy.12 = f32[2048,1024]{1,0:T(8,128)} copy(f32[2048,1024]{0,1:T(8,128)} %convolution_bitcast_fusion.1) | data formatting | bytes 16777216
  135.3 0.0 reduce-scatter.7.cloned.1.call-update
  135.3 0.0 reduce-scatter.9.cloned.1.call-start
  135.3 58.3 %convolution_bitcast_fusion = f32[2048,1024]{0,1:T(8,128)} fusion(f32[2048,768]{1,0:T(8,128)} %all-gather.2.cloned.1.call-done, f32[768,2,1024]{2,0,1:T(8,128)} %copy_select_fusion), kind=kOutput, calls=%fused_computation.1 | convolution fusion | flops 19327352832 | bytes 17825792 | tf_op jit(solution)/shard_map/dot_general | solution.py:29
  193.7 9.3 %copy.14 = f32[2048,1024]{1,0:T(8,128)} copy(f32[2048,1024]{0,1:T(8,128)} %convolution_bitcast_fusion) | data formatting | bytes 16777216
  202.9 0.0 reduce-scatter.9.cloned.1.call-update
  203.0 112.8 %reduce-scatter.7.cloned.1.call-done = f32[64,1024]{1,0:T(8,128)} async-done(((f32[2048,1024]{1,0:T(8,128)}), f32[64,1024]{1,0:T(8,128)}) %reduce-scatter.7.cloned.1.call-update) | async-done | bytes 262160
  315.7 1.1 copy.13
  316.9 180.0 %reduce-scatter.9.cloned.1.call-done = f32[64,1024]{1,0:T(8,128)} async-done(((f32[2048,1024]{1,0:T(8,128)}), f32[64,1024]{1,0:T(8,128)}) %reduce-scatter.9.cloned.1.call-update) | async-done | bytes 262160
  496.9 1.1 copy.15
  498.1 0.1 pad_maximum_fusion
  498.1 1.1 copy.11
  (2 shorter events, 0.0 us)
Async XLA Ops:
  6.5 75.0 %all-gather.2.cloned.1.call-start = ((), (), s32[]{:S(2)}) async-start(), calls=%async_computation.2 | async-start | bytes 7077888 | tf_op jit(solution)/shard_map/all_gather | solution.py:23
  7.3 308.5 %reduce-scatter.7.cloned.1.call-start = ((), (), s32[]{:S(2)}) async-start(), calls=%async_computation.3 | async-start | bytes 8650752
  135.3 361.6 %reduce-scatter.9.cloned.1.call-start = ((), (), s32[]{:S(2)}) async-start(), calls=%async_computation.4 | async-start | bytes 8650752
Sparse Core Ops, SparseCore 0:
  9.2 72.3 all-gather.1
  135.4 180.2 reduce-scatter.6
  318.3 178.5 reduce-scatter.8
where the time goes:
time: 509 us; the launch traced here: 506 us
  waiting for transfers between devices  358 us (70%)
  matrix products  103 us (20%)
  local copies, waits for them, and re-layouts  22 us (4%)
  between operations  13.3 us (3%)
  other arithmetic  9.8 us (2%)
    unnamed x5, waiting for transfers between devices  294 us
    dot_general x2, matrix products, shards(): jnp.dot(gathered, slab_tile, precision=lax.Precision.HIGHEST, preferred_e...  103 us
    all_gather x1, waiting for transfers between devices, shards(): gathered = lax.all_gather(amplitudes, 'narrow', axis=0, tiled=True)  64.5 us
    unnamed x4, local copies, waits for them, and re-layouts  20.8 us
  transfers between devices with their start and end apart: 3, of which 3 were waited for; matrix products, arithmetic and copies ran while one was open for 16% of the time, Pallas kernels for 0%

commit v1 on v0

v1 whole, which is shorter than its diff:
```python
import jax
import jax.numpy as jnp
from jax import lax
from jax.experimental import pallas as pl
from jax.experimental.pallas import tpu as pltpu
from jax.sharding import PartitionSpec as P

MESH = pl.DeviceIdType.MESH


def irrep_labels(positions, sizes):
    block_ends = jnp.cumsum(sizes, axis=-1)
    return jnp.sum((positions[..., None] >= block_ends).astype(jnp.int32), axis=-1)


def ladder_kernel(
    a_ref, bh_ref, bl_ref, out_ref, aall, ahl, p, yr, land, a_s, a_r, y_s, y_r, d_s, d_r
):
    rows, depth = a_ref.shape
    sub = rows // 4
    half = rows // 2
    cols = bh_ref.shape[2]
    w = lax.axis_index("wide")
    n = lax.axis_index("narrow")
    y = lax.rem(w, 4)
    j = lax.div(w, 4)
    x = lax.div(j, 2)
    zl = lax.rem(j, 2)
    zh = lax.div(n, 2)
    c = lax.rem(n, 2)
    right = (j * 4 + lax.rem(y + 1, 4), n)
    left = (j * 4 + lax.rem(y + 3, 4), n)
    zup = (w, lax.rem(zh + 1, 4) * 2 + c)
    zdn = (w, lax.rem(zh + 3, 4) * 2 + c)
    sib = (w, zh * 2 + 1 - c)

    def owner(d):
        return (lax.rem(j + d, 8) * 4 + y, n)

    barrier = pltpu.get_barrier_semaphore()
    for dev in [right, left, zup, zdn, sib] + [owner(d) for d in range(1, 8)]:
        pl.semaphore_signal(barrier, inc=1, device_id=dev, device_id_type=MESH)
    pl.semaphore_wait(barrier, 12)

    def remote(src, dst, ss, rs, dev):
        return pltpu.make_async_remote_copy(
            src_ref=src, dst_ref=dst, send_sem=ss, recv_sem=rs,
            device_id=dev, device_id_type=MESH,
        )

    lo, hi = pl.ds(0, half), pl.ds(half, half)

    def acopy(i):
        src, dst, dev = [
            (a_ref.at[lo], aall.at[0, 3, lo], zup),
            (a_ref.at[hi], aall.at[0, 3, hi], zup),
            (a_ref.at[hi], aall.at[0, 1, hi], zdn),
            (a_ref.at[lo], aall.at[0, 1, lo], zdn),
            (a_ref, aall.at[1, 0], sib),
            (aall.at[0, 3, lo], aall.at[0, 2, lo], zup),
            (aall.at[0, 1, hi], aall.at[0, 2, hi], zdn),
            (aall.at[0, 3], aall.at[1, 3], sib),
            (aall.at[0, 1], aall.at[1, 1], sib),
            (aall.at[0, 2], aall.at[1, 2], sib),
        ][i]
        return remote(src, dst, a_s.at[i], a_r.at[i], dev)

    for i in (4, 0, 2, 1, 3):
        acopy(i).start()
    aall[0, 0] = a_ref[...]

    r_own = lax.rem(x - zh + 4, 4)
    r_last = jnp.where(r_own == 0, 2, r_own)
    r_first = jnp.where(r_own == 1, 3, 1)
    r_mid = 6 - r_last - r_first
    q_last = jnp.where(c == zl, 0, 1)

    def slot(k):
        g = lax.div(k, 2)
        b = lax.rem(k, 2)
        r = jnp.where(g == 0, 0, jnp.where(g == 1, r_first, jnp.where(g == 2, r_mid, r_last)))
        q = jnp.where(g == 0, b, jnp.where(b == 1, q_last, 1 - q_last))
        return r, q

    def distance(k):
        r, q = slot(k)
        block = 2 * lax.rem(zh + r, 4) + jnp.where(q == 0, c, 1 - c)
        return lax.rem(block - j + 8, 8)

    def ring(s, t, k):
        at = lax.rem(y + 3 - t + 4, 4) if s == 0 else lax.rem(y + 1 + t, 4)
        piece = pl.ds(pl.multiple_of(at * sub, sub), sub)
        return piece, remote(
            p.at[s, k, piece], yr.at[s, t, k], y_s.at[s, t, k], y_r.at[s, t, k],
            right if s == 0 else left,
        )

    mine = pl.ds(pl.multiple_of(y * sub, sub), sub)

    def direct(k, d):
        return remote(p.at[:, k, mine], land.at[d], d_s.at[d], d_r.at[d], owner(d))

    def pass_on(t, k):
        for s in range(2):
            ring(s, t - 1, k)[1].wait_recv()
            piece, copy = ring(s, t, k)
            p[s, k, piece, :] += yr[s, t - 1, k]
            copy.start()

    def finish(k):
        for s in range(2):
            ring(s, 2, k)[1].wait_recv()
            p[s, k, mine, :] += yr[s, 2, k]
        d = distance(k)

        @pl.when(d != 0)
        def _():
            direct(k, d).start()

    def compute(k):
        r, q = slot(k)
        a = aall[q, r]
        ah = a.astype(jnp.bfloat16)
        ahl[0:rows] = ah
        ahl[rows:] = (a - ah.astype(jnp.float32)).astype(jnp.bfloat16)
        width = 512
        per = cols // width
        for s in range(2):
            def tile(ci, _):
                cs = pl.ds(pl.multiple_of(ci * width, width), width)
                u = jnp.dot(ahl[...], bh_ref[s, :, cs], preferred_element_type=jnp.float32)
                v = jnp.dot(ahl[0:rows], bl_ref[s, :, cs], preferred_element_type=jnp.float32)
                p[s, k, :, cs] = u[:rows] + (u[rows:] + v)
                return 0

            lax.fori_loop(0, per, tile, 0)
            ring(s, 0, k)[1].start()

    def body(i, _):
        @pl.when(i >= 3)
        def _():
            finish(i - 3)

        @pl.when((i >= 2) & (i < 10))
        def _():
            pass_on(2, i - 2)

        @pl.when((i >= 1) & (i < 9))
        def _():
            pass_on(1, i - 1)

        @pl.when(i == 1)
        def _():
            acopy(4).wait_recv()

        @pl.when(i == 2)
        def _():
            acopy(0).wait_recv()
            acopy(5).start()
            acopy(2).wait_recv()
            acopy(6).start()
            acopy(1).wait_recv()
            acopy(7).start()
            acopy(3).wait_recv()
            acopy(8).start()
            acopy(7).wait_recv()
            acopy(8).wait_recv()

        @pl.when(i == 4)
        def _():
            acopy(5).wait_recv()
            acopy(6).wait_recv()
            acopy(9).start()
            acopy(9).wait_recv()

        @pl.when(i < 8)
        def _():
            compute(i)

        return 0

    lax.fori_loop(0, 11, body, 0)

    k_own = 0
    for k in range(8):
        k_own = k_own + jnp.where(distance(k) == 0, k, 0)
    out_ref[...] = p[:, k_own, mine, :]
    for d in range(1, 8):
        direct(0, d).wait_recv()
        out_ref[...] += land[d]
    for d in range(1, 8):
        direct(0, d).wait_send()
    for i in range(10):
        acopy(i).wait_send()

    def drain(k, _):
        for s in range(2):
            for t in range(3):
                ring(s, t, k)[1].wait_send()
        return 0

    lax.fori_loop(0, 8, drain, 0)


def shards(amplitudes, integrals, ab_sizes, cd_sizes):
    pair_rows, slab_count, slab_cols = integrals.shape
    block = amplitudes.shape[0]
    ab_positions = lax.axis_index("wide") * pair_rows + lax.iota(jnp.int32, pair_rows)
    cd_positions = lax.axis_index("narrow") * slab_cols + lax.iota(jnp.int32, slab_cols)
    ab_label = irrep_labels(ab_positions, ab_sizes)
    cd_label = irrep_labels(cd_positions[None, :], cd_sizes[:, None, :])
    masked = jnp.where(
        ab_label[None, :, None] == cd_label[:, None, :],
        jnp.transpose(integrals, (1, 0, 2)),
        jnp.zeros((), integrals.dtype),
    )
    top = lax.reduce_precision(masked, 8, 7)
    high = top.astype(jnp.bfloat16)
    low = (masked - top).astype(jnp.bfloat16)
    f32 = jnp.float32
    vmem = pl.BlockSpec(memory_space=pltpu.VMEM)
    result = pl.pallas_call(
        ladder_kernel,
        out_shape=jax.ShapeDtypeStruct((slab_count, block // 4, slab_cols), f32),
        in_specs=[vmem] * 3,
        out_specs=vmem,
        scratch_shapes=[
            pltpu.VMEM((2, 4, block, pair_rows), f32),
            pltpu.VMEM((2 * block, pair_rows), jnp.bfloat16),
            pltpu.VMEM((2, 8, block, slab_cols), f32),
            pltpu.VMEM((2, 3, 8, block // 4, slab_cols), f32),
            pltpu.VMEM((8, 2, block // 4, slab_cols), f32),
            pltpu.SemaphoreType.DMA((10,)),
            pltpu.SemaphoreType.DMA((10,)),
            pltpu.SemaphoreType.DMA((2, 3, 8)),
            pltpu.SemaphoreType.DMA((2, 3, 8)),
            pltpu.SemaphoreType.DMA((8,)),
            pltpu.SemaphoreType.DMA((8,)),
        ],
        compiler_params=pltpu.CompilerParams(
            collective_id=0, has_side_effects=True, vmem_limit_bytes=60 * 2**20
        ),
        cost_estimate=pl.CostEstimate(
            flops=6 * 2048 * 768 * 2048, bytes_accessed=16 * 2**20, transcendentals=0
        ),
    )(amplitudes, high, low)
    return jnp.transpose(result, (1, 0, 2))


def solution(mesh):
    return jax.shard_map(
        shards,
        mesh=mesh,
        in_specs=(P("narrow", "wide"), P("wide", None, "narrow"), P(), P()),
        out_specs=P("wide", None, "narrow"),
        check_vma=False,
    )
```

time: 509 us -> 199 us (0.39)
  the two profiles are of different devices: /device:TPU:64 before, /device:TPU:36 now
where the time goes in v1:
time: 199 us
  Pallas kernels  187 us (94%)
  other arithmetic  9.35 us (5%)
  local copies, waits for them, and re-layouts  2.24 us (1%)
    pallas_call x1, Pallas kernels, shards(): pl.pallas_call(ladder_kernel, out_shape=jax.ShapeDtypeStruct((slab_count,...  187 us
    convert_element_type x1, other arithmetic, shards(): low = (masked - top).astype(jnp.bfloat16)  7.48 us

profile of v1, /device:TPU:36, one launch (start us, length us, event | category | flops | bytes accessed | tf_op | source)
XLA Modules:
  0.0 198.7 jit_solution(1137254674573436112)
XLA Ops:
  0.0 0.8 reduce-window.8
  0.8 0.9 reduce_window_sum.18
  1.7 0.1 convert_reduce_fusion.1
  1.8 0.1 convert_reduce_fusion
  1.9 7.5 %fusion = (bf16[2,768,1024]{2,1,0:T(8,128)(2,1)}, bf16[2,768,1024]{2,1,0:T(8,128)(2,1)}) fusion(f32[768,2,1024]{2,1,0:T(2,128)} %param.5, s32[2,1024]{1,0:T(2,128)S(1)} %convert_reduce_fusion, s32[768]{0:T(1024)S(1)} %convert_reduce_fusion.1), kind=kLoop, calls=%fused_computation.2 | loop fusion | flops 9437184 | bytes 12594176 | tf_op jit(solution)/shard_map/convert_element_type | solution.py:219
  9.4 187.0 %shard_map.46 = f32[2,64,1024]{2,1,0:T(8,128)} custom-call(f32[256,768]{1,0:T(8,128)} %a_ref.1, bf16[2,768,1024]{2,1,0:T(8,128)(2,1)} %get-tuple-element.6.bh_ref, bf16[2,768,1024]{2,1,0:T(8,128)(2,1)} %get-tuple-element.5.bl_ref), custom_call_target="tpu_custom_call" | custom-call | flops 19327352832 | bytes 16777216 | tf_op jit(solution)/shard_map/pallas_call | solution.py:222
  196.4 2.2 %copy.8 = f32[64,2,1024]{2,1,0:T(2,128)} copy(f32[64,2,1024]{2,0,1:T(8,128)} %bitcast.9) | data formatting | bytes 1048576 | tf_op jit(solution)/shard_map/transpose | solution.py:247
  (2 shorter events, 0.0 us)

commit v2 on v1

v2 whole, which is shorter than its diff:
```python
import jax
import jax.numpy as jnp
from jax import lax
from jax.experimental import pallas as pl
from jax.experimental.pallas import tpu as pltpu
from jax.sharding import PartitionSpec as P

MESH = pl.DeviceIdType.MESH
LANES = 128
SIDE = 256


def ladder_kernel(
    a_ref, b_hbm, ab_ref, cd_ref, out_ref,
    aall, ahl, braw, bh, bl, rowlab, py, px, yr, land, xl, zl2,
    b_sem, a_s, a_r, y_s, y_r, d_s, d_r, x_s, x_r, z_s, z_r,
):
    rows, depth = a_ref.shape
    sub = rows // 4
    half = rows // 2
    cols = bh.shape[2]
    main = cols - SIDE
    tiles = cols // LANES
    w = lax.axis_index("wide")
    n = lax.axis_index("narrow")
    y = lax.rem(w, 4)
    j = lax.div(w, 4)
    x = lax.div(j, 2)
    zl = lax.rem(j, 2)
    zh = lax.div(n, 2)
    c = lax.rem(n, 2)
    right = (j * 4 + lax.rem(y + 1, 4), n)
    left = (j * 4 + lax.rem(y + 3, 4), n)
    zup = (w, lax.rem(zh + 1, 4) * 2 + c)
    zdn = (w, lax.rem(zh + 3, 4) * 2 + c)
    sib = (w, zh * 2 + 1 - c)

    def owner(d):
        return (lax.rem(j + d, 8) * 4 + y, n)

    def plane(eb, dy):
        return ((2 * x + lax.rem(zl + eb, 2)) * 4 + lax.rem(y + dy, 4), n)

    load_b = pltpu.make_async_copy(b_hbm, braw, b_sem)
    load_b.start()

    partners = [right, left, zup, zdn, sib, plane(0, 2)]
    partners += [owner(d) for d in range(1, 8)] + [plane(1, dy) for dy in range(1, 4)]
    barrier = pltpu.get_barrier_semaphore()
    for dev in partners:
        pl.semaphore_signal(barrier, inc=1, device_id=dev, device_id_type=MESH)
    pl.semaphore_wait(barrier, len(partners))

    def remote(src, dst, ss, rs, dev):
        return pltpu.make_async_remote_copy(
            src_ref=src, dst_ref=dst, send_sem=ss, recv_sem=rs,
            device_id=dev, device_id_type=MESH,
        )

    hc = pl.ds(pl.multiple_of(c * half, half), half)

    def acopy(i):
        src, dst, dev = [
            (a_ref, aall.at[0, c], sib),
            (aall.at[0, 0, hc], aall.at[3, 0, hc], zup),
            (aall.at[0, 1, hc], aall.at[3, 1, hc], zup),
            (aall.at[3, 0, hc], aall.at[2, 0, hc], zup),
            (aall.at[0, 1, hc], aall.at[1, 1, hc], zdn),
            (aall.at[0, 0, hc], aall.at[1, 0, hc], zdn),
            (aall.at[1, 1, hc], aall.at[2, 1, hc], zdn),
            (aall.at[3, 0, hc], aall.at[3, 0, hc], sib),
            (aall.at[1, 1, hc], aall.at[1, 1, hc], sib),
            (aall.at[3, 1, hc], aall.at[3, 1, hc], sib),
            (aall.at[1, 0, hc], aall.at[1, 0, hc], sib),
            (aall.at[2, 0, hc], aall.at[2, 0, hc], sib),
            (aall.at[2, 1, hc], aall.at[2, 1, hc], sib),
        ][i]
        return remote(src, dst, a_s.at[i], a_r.at[i], dev)

    def arrived(*which):
        for i in which:
            if i == 0:
                remote(a_ref, aall.at[0, 1 - c], a_s.at[0], a_r.at[0], sib).wait_recv()
            elif i >= 7:
                r, bit = [(3, 0), (1, 1), (3, 1), (1, 0), (2, 0), (2, 1)][i - 7]
                ho = pl.ds(pl.multiple_of((1 - c) * half, half), half)
                part = aall.at[r, bit, ho]
                remote(part, part, a_s.at[i], a_r.at[i], sib).wait_recv()
            else:
                acopy(i).wait_recv()

    def begin(*which):
        for i in which:
            acopy(i).start()

    begin(0)
    aall[0, c] = a_ref[...]
    arrived(0)
    begin(1, 4, 2, 5)

    def labels(at, ends):
        total = jnp.zeros(at.shape, jnp.int32)
        for end in ends:
            total += (at >= end).astype(jnp.int32)
        return total

    def running(values):
        ends = []
        for v in values:
            ends.append(v + ends[-1] if ends else v)
        return ends

    ab_ends = running([ab_ref[h] for h in range(8)])
    chunk = 64

    def row_labels(i, _):
        at = pl.ds(pl.multiple_of(i * chunk, chunk), chunk)
        first = w * depth + i * chunk
        rowlab[at, :] = labels(first + lax.broadcasted_iota(jnp.int32, (chunk, LANES), 0), ab_ends)
        return 0

    lax.fori_loop(0, depth // chunk, row_labels, 0)
    load_b.wait()
    for s in range(2):
        cd_ends = running([cd_ref[s, h] for h in range(8)])

        def split_tile(t, _):
            first = n * cols + t * LANES
            col = labels(first + lax.broadcasted_iota(jnp.int32, (8, LANES), 1), cd_ends)[0:1]
            raw = braw[pl.ds(2 * t + s, depth, stride=2 * tiles), :]
            m = jnp.where(rowlab[...] == col, raw, 0.0)
            h = m.astype(jnp.bfloat16)
            at = pl.ds(pl.multiple_of(t * LANES, LANES), LANES)
            bh[s, :, at] = h
            bl[s, :, at] = (m - h.astype(jnp.float32)).astype(jnp.bfloat16)
            return 0

        lax.fori_loop(0, tiles, split_tile, 0)

    r_own = lax.rem(x - zh + 4, 4)
    r_last = jnp.where(r_own == 0, 2, r_own)
    r_first = jnp.where(r_own == 3, 1, 3)
    r_mid = 6 - r_last - r_first

    def slot(k):
        g = lax.div(k, 2)
        b = lax.rem(k, 2)
        r = jnp.where(g == 0, 0, jnp.where(g == 1, r_first, jnp.where(g == 2, r_mid, r_last)))
        start = jnp.where(g == 0, c, jnp.where(g == 3, 1 - zl, jnp.where(r == 3, 0, 1)))
        return r, jnp.where(b == 0, start, 1 - start)

    def slot_of(r, bit):
        found = 0
        for k in range(8):
            rk, bk = slot(k)
            found = found + jnp.where((rk == r) & (bk == bit), k, 0)
        return found

    def ring(s, t, k):
        at = lax.rem(y + 7 - t, 4) if s == 0 else lax.rem(y + 1 + t, 4)
        piece = pl.ds(pl.multiple_of(at * sub, sub), sub)
        return piece, remote(
            py.at[s, k, piece], yr.at[s, t, k], y_s.at[s, t, k], y_r.at[s, t, k],
            right if s == 0 else left,
        )

    mine = pl.ds(pl.multiple_of(y * sub, sub), sub)

    def direct(k, d):
        return remote(py.at[:, k, mine], land.at[d], d_s.at[d], d_r.at[d], owner(d))

    def sideways(k, dx, bit):
        dev = ((2 * lax.rem(x + dx, 4) + zl) * 4 + y, n)
        return remote(px.at[k], xl.at[dx, bit], x_s.at[dx, bit], x_r.at[dx, bit], dev)

    def spread(k, eb, dy):
        e = eb * 4 + dy
        piece = pl.ds(pl.multiple_of(lax.rem(y + dy, 4) * sub, sub), sub)
        return remote(px.at[k, :, piece], zl2.at[e], z_s.at[e], z_r.at[e], plane(eb, dy))

    def pass_on(t, k):
        for s in range(2):
            ring(s, t - 1, k)[1].wait_recv()
            piece, copy = ring(s, t, k)
            py[s, k, piece, :] += yr[s, t - 1, k]
            copy.start()

    def finish(k):
        for s in range(2):
            ring(s, 2, k)[1].wait_recv()
            py[s, k, mine, :] += yr[s, 2, k]
        r, bit = slot(k)
        d = lax.rem(2 * lax.rem(zh + r, 4) + bit - j + 8, 8)

        @pl.when(d != 0)
        def _():
            direct(k, d).start()

    width = 512

    def compute(k):
        r, bit = slot(k)
        a = aall[r, bit]
        ah = a.astype(jnp.bfloat16)
        ahl[0:rows] = ah
        ahl[rows:] = (a - ah.astype(jnp.float32)).astype(jnp.bfloat16)
        for s in range(2):
            for lo in range(0, cols, width):
                cs = slice(lo, lo + width)
                u = jnp.dot(ahl[...], bh[s, :, cs], preferred_element_type=jnp.float32)
                v = jnp.dot(ahl[0:rows], bl[s, :, cs], preferred_element_type=jnp.float32)
                total = u[:rows] + (u[rows:] + v)
                if lo + width <= main:
                    py[s, k, :, cs] = total
                else:
                    py[s, k, :, lo:main] = total[:, : main - lo]
                    px[k, s] = total[:, main - lo :]
            ring(s, 0, k)[1].start()
        dx = lax.rem(r - r_own + 4, 4)

        @pl.when(dx != 0)
        def _():
            sideways(k, dx, bit).start()

    def gather_side():
        for eb in range(2):
            bit = lax.rem(zl + eb, 2)
            k = slot_of(r_own, bit)
            for dx in range(1, 4):
                sideways(k, dx, bit).wait_recv()
            for dy in range(4):
                piece = pl.ds(pl.multiple_of(lax.rem(y + dy, 4) * sub, sub), sub)
                px[k, :, piece, :] += (
                    xl[1, bit, :, piece, :] + xl[2, bit, :, piece, :] + xl[3, bit, :, piece, :]
                )
                if eb + dy:
                    spread(k, eb, dy).start()

    def body(i, _):
        @pl.when(i >= 3)
        def _():
            finish(i - 3)

        @pl.when((i >= 2) & (i < 10))
        def _():
            pass_on(2, i - 2)

        @pl.when((i >= 1) & (i < 9))
        def _():
            pass_on(1, i - 1)

        @pl.when(i == 2)
        def _():
            arrived(1, 4)
            begin(3, 6, 7, 8)
            arrived(7, 8)

        @pl.when(i == 3)
        def _():
            arrived(2, 5)
            begin(9, 10)
            arrived(9, 10)

        @pl.when(i == 4)
        def _():
            arrived(3, 6)
            begin(11, 12)
            arrived(11, 12)

        @pl.when(i < 8)
        def _():
            compute(i)

        @pl.when(i == 8)
        def _():
            gather_side()

        return 0

    lax.fori_loop(0, 11, body, 0)

    k_own = slot_of(r_own, zl)
    out_ref[:, :, :main] = py[:, k_own, mine, :]
    out_ref[:, :, main:] = px[k_own, :, mine, :]
    for e in range(1, 8):
        spread(k_own, e // 4, e % 4).wait_recv()
        out_ref[:, :, main:] += zl2[e]
    for d in range(1, 8):
        direct(0, d).wait_recv()
        out_ref[:, :, :main] += land[d]
    for d in range(1, 8):
        direct(0, d).wait_send()
        spread(k_own, d // 4, d % 4).wait_send()
    for dx in range(1, 4):
        for bit in range(2):
            sideways(0, dx, bit).wait_send()
    for i in range(13):
        acopy(i).wait_send()

    def drain(k, _):
        for s in range(2):
            for t in range(3):
                ring(s, t, k)[1].wait_send()
        return 0

    lax.fori_loop(0, 8, drain, 0)


def shards(amplitudes, integrals, ab_sizes, cd_sizes):
    depth, slabs, cols = integrals.shape
    rows = amplitudes.shape[0]
    sub = rows // 4
    main = cols - SIDE
    tiles = cols // LANES
    f32 = jnp.float32
    bf16 = jnp.bfloat16
    dma = pltpu.SemaphoreType.DMA
    flat = jnp.transpose(integrals.reshape(depth, slabs, tiles, LANES), (0, 2, 1, 3))
    flat = flat.reshape(depth * tiles * slabs, LANES)
    vmem = pl.BlockSpec(memory_space=pltpu.VMEM)
    smem = pl.BlockSpec(memory_space=pltpu.SMEM)
    result = pl.pallas_call(
        ladder_kernel,
        out_shape=jax.ShapeDtypeStruct((slabs, sub, cols), f32),
        in_specs=[vmem, pl.BlockSpec(memory_space=pl.ANY), smem, smem],
        out_specs=vmem,
        scratch_shapes=[
            pltpu.VMEM((4, 2, rows, depth), f32),
            pltpu.VMEM((2 * rows, depth), bf16),
            pltpu.VMEM(flat.shape, f32),
            pltpu.VMEM((slabs, depth, cols), bf16),
            pltpu.VMEM((slabs, depth, cols), bf16),
            pltpu.VMEM((depth, LANES), jnp.int32),
            pltpu.VMEM((slabs, 8, rows, main), f32),
            pltpu.VMEM((8, slabs, rows, SIDE), f32),
            pltpu.VMEM((slabs, 3, 8, sub, main), f32),
            pltpu.VMEM((8, slabs, sub, main), f32),
            pltpu.VMEM((4, 2, slabs, rows, SIDE), f32),
            pltpu.VMEM((8, slabs, sub, SIDE), f32),
            dma(()),
            dma((13,)), dma((13,)),
            dma((slabs, 3, 8)), dma((slabs, 3, 8)),
            dma((8,)), dma((8,)),
            dma((4, 2)), dma((4, 2)),
            dma((8,)), dma((8,)),
        ],
        compiler_params=pltpu.CompilerParams(
            collective_id=0, has_side_effects=True, vmem_limit_bytes=62 * 2**20
        ),
        cost_estimate=pl.CostEstimate(
            flops=6 * 8 * rows * depth * slabs * cols, bytes_accessed=8 * 2**20, transcendentals=0
        ),
    )(amplitudes, flat, ab_sizes, cd_sizes)
    return jnp.transpose(result, (1, 0, 2))


def solution(mesh):
    return jax.shard_map(
        shards,
        mesh=mesh,
        in_specs=(P("narrow", "wide"), P("wide", None, "narrow"), P(), P()),
        out_specs=P("wide", None, "narrow"),
        check_vma=False,
    )
```

time: 199 us -> 169 us (0.85)
  the two profiles are of different devices: /device:TPU:36 before, /device:TPU:12 now
where the time goes in v2:
time: 169 us; the launch traced here: 168 us
  Pallas kernels  166 us (98%)
  local copies, waits for them, and re-layouts  2.24 us (1%)
    pallas_call x1, Pallas kernels, shards(): pl.pallas_call(ladder_kernel, out_shape=jax.ShapeDtypeStruct((slabs, sub,...  166 us

profile of v2, /device:TPU:12, one launch (start us, length us, event | category | flops | bytes accessed | tf_op | source)
XLA Modules:
  0.0 168.4 jit_solution(8079377954434653250)
XLA Ops:
  0.0 166.2 %shard_map.46 = f32[2,64,1024]{2,1,0:T(8,128)} custom-call(f32[256,768]{1,0:T(8,128)} %a_ref.1, f32[12288,128]{1,0:T(8,128)} %bitcast.7, s32[8]{0:T(128)} %ab_ref.1, s32[2,8]{1,0:T(2,128)} %cd_ref.1), custom_call_target="tpu_custom_call" | custom-call | flops 19327352832 | bytes 8388608 | tf_op jit(solution)/shard_map/pallas_call | solution.py:322
  166.2 2.2 %copy.6 = f32[64,2,1024]{2,1,0:T(2,128)} copy(f32[64,2,1024]{2,0,1:T(8,128)} %bitcast.6) | data formatting | bytes 1048576 | tf_op jit(solution)/shard_map/transpose | solution.py:354

commit v3 on v2

--- a/solution.py
+++ b/solution.py
@@ -1,3 +1,5 @@
+import functools
+
 import jax
 import jax.numpy as jnp
 from jax import lax
@@ -12,8 +14,8 @@
 
 def ladder_kernel(
     a_ref, b_hbm, ab_ref, cd_ref, out_ref,
-    aall, ahl, braw, bh, bl, rowlab, py, px, yr, land, xl, zl2,
-    b_sem, a_s, a_r, y_s, y_r, d_s, d_r, x_s, x_r, z_s, z_r,
+    aall, ahl, braw, bh, bl, rowlab, py, px, yr, xp, xl, rp, rl, zr, zl2,
+    b_sem, a_s, a_r, y_s, y_r, p_s, p_r, l_s, l_r, z_s, z_r,
 ):
     rows, depth = a_ref.shape
     sub = rows // 4
@@ -35,8 +37,8 @@
     zdn = (w, lax.rem(zh + 3, 4) * 2 + c)
     sib = (w, zh * 2 + 1 - c)
 
-    def owner(d):
-        return (lax.rem(j + d, 8) * 4 + y, n)
+    xup = ((2 * lax.rem(x + 1, 4) + zl) * 4 + y, n)
+    xdn = ((2 * lax.rem(x + 3, 4) + zl) * 4 + y, n)
 
     def plane(eb, dy):
         return ((2 * x + lax.rem(zl + eb, 2)) * 4 + lax.rem(y + dy, 4), n)
@@ -44,8 +46,8 @@
     load_b = pltpu.make_async_copy(b_hbm, braw, b_sem)
     load_b.start()
 
-    partners = [right, left, zup, zdn, sib, plane(0, 2)]
-    partners += [owner(d) for d in range(1, 8)] + [plane(1, dy) for dy in range(1, 4)]
+    partners = [right, left, zup, zdn, sib, xup, xdn, plane(0, 2)]
+    partners += [plane(1, dy) for dy in range(4)]
     barrier = pltpu.get_barrier_semaphore()
     for dev in partners:
         pl.semaphore_signal(barrier, inc=1, device_id=dev, device_id_type=MESH)
@@ -96,7 +98,7 @@
     begin(0)
     aall[0, c] = a_ref[...]
     arrived(0)
-    begin(1, 4, 2, 5)
+    begin(1, 4)
 
     def labels(at, ends):
         total = jnp.zeros(at.shape, jnp.int32)
@@ -120,8 +122,7 @@
         return 0
 
     lax.fori_loop(0, depth // chunk, row_labels, 0)
-    load_b.wait()
-    for s in range(2):
+    def split_slab(s):
         cd_ends = running([cd_ref[s, h] for h in range(8)])
 
         def split_tile(t, _):
@@ -138,16 +139,14 @@
         lax.fori_loop(0, tiles, split_tile, 0)
 
     r_own = lax.rem(x - zh + 4, 4)
-    r_last = jnp.where(r_own == 0, 2, r_own)
-    r_first = jnp.where(r_own == 3, 1, 3)
-    r_mid = 6 - r_last - r_first
 
     def slot(k):
-        g = lax.div(k, 2)
-        b = lax.rem(k, 2)
-        r = jnp.where(g == 0, 0, jnp.where(g == 1, r_first, jnp.where(g == 2, r_mid, r_last)))
-        start = jnp.where(g == 0, c, jnp.where(g == 3, 1 - zl, jnp.where(r == 3, 0, 1)))
-        return r, jnp.where(b == 0, start, 1 - start)
+        far = (k == 5) | (k == 7)
+        near = (k == 3) | (k == 4)
+        r = jnp.where(k < 2, 0, jnp.where(far, 2, jnp.where(near, 1, 3)))
+        bit = jnp.where(near, 4 - k, lax.div(k, 4))
+        bit = jnp.where(far, jnp.where(k == 7, zl, 1 - zl), bit)
+        return r, jnp.where(k < 2, lax.rem(k + c, 2), bit)
 
     def slot_of(r, bit):
         found = 0
@@ -166,12 +165,68 @@
 
     mine = pl.ds(pl.multiple_of(y * sub, sub), sub)
 
-    def direct(k, d):
-        return remote(py.at[:, k, mine], land.at[d], d_s.at[d], d_r.at[d], owner(d))
-
-    def sideways(k, dx, bit):
-        dev = ((2 * lax.rem(x + dx, 4) + zl) * 4 + y, n)
-        return remote(px.at[k], xl.at[dx, bit], x_s.at[dx, bit], x_r.at[dx, bit], dev)
+    def data(kind, k, s):
+        return py.at[s, k, mine] if kind else px.at[k, s]
+
+    def handed(kind, k, e, bit):
+        dst = (rp if kind else xp).at[e, bit]
+        sems = p_s.at[kind, e, bit], p_r.at[kind, e, bit]
+        return remote(data(kind, k, e), dst, *sems, xdn if e else xup)
+
+    def landing(kind, k, f, bit, s):
+        dst = (rl if kind else xl).at[f, bit, s]
+        sems = l_s.at[kind, f, bit, s], l_r.at[kind, f, bit, s]
+        return remote(data(kind, k, s), dst, *sems, xdn if f else xup)
+
+    def towards(k):
+        r, bit = slot(k)
+        return lax.rem(r - r_own + 4, 4), bit
+
+    def hand_out(kind, k):
+        dx, bit = towards(k)
+
+        @pl.when(dx == 2)
+        def _():
+            for e in range(2):
+                handed(kind, k, e, bit).start()
+
+        for f in range(2):
+            @pl.when(dx == 1 + 2 * f)
+            def _():
+                landing(kind, k, f, bit, 1 - f).start()
+
+    def relay(kind, k):
+        dx, bit = towards(k)
+        for f in range(2):
+            @pl.when(dx == 1 + 2 * f)
+            def _():
+                handed(kind, k, f, bit).wait_recv()
+                if kind:
+                    py[f, k, mine, :] += rp[f, bit]
+                else:
+                    px[k, f] += xp[f, bit]
+                landing(kind, k, f, bit, f).start()
+
+    def landed(kind, k, bit):
+        for f in range(2):
+            for s in range(2):
+                landing(kind, k, f, bit, s).wait_recv()
+
+    def across(k):
+        return remote(py.at[:, k, mine], zr, z_s.at[0], z_r.at[0], plane(1, 0))
+
+    def collect(k):
+        dx, bit = towards(k)
+
+        @pl.when(dx == 0)
+        def _():
+            landed(1, k, bit)
+            for s in range(2):
+                py[s, k, mine, :] += rl[0, bit, s] + rl[1, bit, s]
+
+            @pl.when(bit != zl)
+            def _():
+                across(k).start()
 
     def spread(k, eb, dy):
         e = eb * 4 + dy
@@ -189,68 +244,92 @@
         for s in range(2):
             ring(s, 2, k)[1].wait_recv()
             py[s, k, mine, :] += yr[s, 2, k]
-        r, bit = slot(k)
-        d = lax.rem(2 * lax.rem(zh + r, 4) + bit - j + 8, 8)
-
-        @pl.when(d != 0)
-        def _():
-            direct(k, d).start()
+        hand_out(1, k)
 
     width = 512
 
-    def compute(k):
+    def split_rows(k):
         r, bit = slot(k)
         a = aall[r, bit]
         ah = a.astype(jnp.bfloat16)
         ahl[0:rows] = ah
         ahl[rows:] = (a - ah.astype(jnp.float32)).astype(jnp.bfloat16)
+
+    def compute_slab(k, s):
+        for lo in range(0, cols, width):
+            cs = slice(lo, lo + width)
+            u = jnp.dot(ahl[...], bh[s, :, cs], preferred_element_type=jnp.float32)
+            v = jnp.dot(ahl[0:rows], bl[s, :, cs], preferred_element_type=jnp.float32)
+            total = u[:rows] + (u[rows:] + v)
+            if lo + width <= main:
+                py[s, k, :, cs] = total
+            else:
+                py[s, k, :, lo:main] = total[:, : main - lo]
+                px[k, s] = total[:, main - lo :]
+
+    def compute(k):
+        split_rows(k)
         for s in range(2):
-            for lo in range(0, cols, width):
-                cs = slice(lo, lo + width)
-                u = jnp.dot(ahl[...], bh[s, :, cs], preferred_element_type=jnp.float32)
-                v = jnp.dot(ahl[0:rows], bl[s, :, cs], preferred_element_type=jnp.float32)
-                total = u[:rows] + (u[rows:] + v)
-                if lo + width <= main:
-                    py[s, k, :, cs] = total
-                else:
-                    py[s, k, :, lo:main] = total[:, : main - lo]
-                    px[k, s] = total[:, main - lo :]
-            ring(s, 0, k)[1].start()
-        dx = lax.rem(r - r_own + 4, 4)
-
-        @pl.when(dx != 0)
-        def _():
-            sideways(k, dx, bit).start()
-
-    def gather_side():
-        for eb in range(2):
-            bit = lax.rem(zl + eb, 2)
-            k = slot_of(r_own, bit)
-            for dx in range(1, 4):
-                sideways(k, dx, bit).wait_recv()
+            compute_slab(k, s)
+        hand_out(0, k)
+
+    def gather_side(k):
+        dx, bit = towards(k)
+
+        @pl.when(dx == 0)
+        def _():
+            landed(0, k, bit)
+            eb = lax.rem(bit - zl + 2, 2)
             for dy in range(4):
                 piece = pl.ds(pl.multiple_of(lax.rem(y + dy, 4) * sub, sub), sub)
-                px[k, :, piece, :] += (
-                    xl[1, bit, :, piece, :] + xl[2, bit, :, piece, :] + xl[3, bit, :, piece, :]
-                )
-                if eb + dy:
+                px[k, :, piece, :] += xl[0, bit, :, piece, :] + xl[1, bit, :, piece, :]
+                if dy:
                     spread(k, eb, dy).start()
+                else:
+                    @pl.when(eb != 0)
+                    def _():
+                        spread(k, eb, 0).start()
+
+    def send_first(k):
+        for s in range(2):
+            ring(s, 0, k)[1].start()
+
+    split_rows(0)
+    load_b.wait()
+    for s in range(2):
+        split_slab(s)
+        compute_slab(0, s)
+        ring(s, 0, 0)[1].start()
+    hand_out(0, 0)
 
     def body(i, _):
-        @pl.when(i >= 3)
-        def _():
-            finish(i - 3)
-
-        @pl.when((i >= 2) & (i < 10))
-        def _():
-            pass_on(2, i - 2)
-
-        @pl.when((i >= 1) & (i < 9))
-        def _():
-            pass_on(1, i - 1)
-
-        @pl.when(i == 2)
-        def _():
+        def stages(*which):
+            for late, what in which:
+                @pl.when((i >= late) & (i < late + 8))
+                def _():
+                    what(i - late)
+
+        @pl.when((i > 0) & (i < 8))
+        def _():
+            send_first(i)
+
+        @pl.when(i != 2)
+        def _():
+            stages(
+                (1, functools.partial(pass_on, 1)),
+                (2, functools.partial(pass_on, 2)),
+            )
+
+        stages((3, finish))
+
+        @pl.when(i == 1)
+        def _():
+            pass_on(1, 1)
+            acopy(1).wait_send()
+            begin(2)
+            acopy(4).wait_send()
+            begin(5)
+            pass_on(2, 0)
             arrived(1, 4)
             begin(3, 6, 7, 8)
             arrived(7, 8)
@@ -267,17 +346,16 @@
             begin(11, 12)
             arrived(11, 12)
 
-        @pl.when(i < 8)
-        def _():
-            compute(i)
-
-        @pl.when(i == 8)
-        def _():
-            gather_side()
-
+        stages(
+            (-1, compute),
+            (1, functools.partial(relay, 0)),
+            (4, functools.partial(relay, 1)),
+            (3, gather_side),
+            (5, collect),
+        )
         return 0
 
-    lax.fori_loop(0, 11, body, 0)
+    lax.fori_loop(0, 13, body, 0)
 
     k_own = slot_of(r_own, zl)
     out_ref[:, :, :main] = py[:, k_own, mine, :]
@@ -285,16 +363,18 @@
     for e in range(1, 8):
         spread(k_own, e // 4, e % 4).wait_recv()
         out_ref[:, :, main:] += zl2[e]
-    for d in range(1, 8):
-        direct(0, d).wait_recv()
-        out_ref[:, :, :main] += land[d]
-    for d in range(1, 8):
-        direct(0, d).wait_send()
-        spread(k_own, d // 4, d % 4).wait_send()
-    for dx in range(1, 4):
-        for bit in range(2):
-            sideways(0, dx, bit).wait_send()
-    for i in range(13):
+    across(k_own).wait_recv()
+    out_ref[:, :, :main] += zr[...]
+    across(k_own).wait_send()
+    for e in range(1, 8):
+        spread(k_own, e // 4, e % 4).wait_send()
+    for kind in range(2):
+        for f in range(2):
+            for bit in range(2):
+                handed(kind, 0, f, bit).wait_send()
+                for s in range(2):
+                    landing(kind, 0, f, bit, s).wait_send()
+    for i in (0, 2, 3) + tuple(range(5, 13)):
         acopy(i).wait_send()
 
     def drain(k, _):
@@ -334,14 +414,17 @@
             pltpu.VMEM((slabs, 8, rows, main), f32),
             pltpu.VMEM((8, slabs, rows, SIDE), f32),
             pltpu.VMEM((slabs, 3, 8, sub, main), f32),
-            pltpu.VMEM((8, slabs, sub, main), f32),
-            pltpu.VMEM((4, 2, slabs, rows, SIDE), f32),
+            pltpu.VMEM((2, 2, rows, SIDE), f32),
+            pltpu.VMEM((2, 2, slabs, rows, SIDE), f32),
+            pltpu.VMEM((2, 2, sub, main), f32),
+            pltpu.VMEM((2, 2, slabs, sub, main), f32),
+            pltpu.VMEM((slabs, sub, main), f32),
             pltpu.VMEM((8, slabs, sub, SIDE), f32),
             dma(()),
             dma((13,)), dma((13,)),
             dma((slabs, 3, 8)), dma((slabs, 3, 8)),
-            dma((8,)), dma((8,)),
-            dma((4, 2)), dma((4, 2)),
+            dma((2, 2, 2)), dma((2, 2, 2)),
+            dma((2, 2, 2, 2)), dma((2, 2, 2, 2)),
             dma((8,)), dma((8,)),
         ],
         compiler_params=pltpu.CompilerParams(

time: 169 us -> 161 us (0.953)
  the two profiles are of different devices: /device:TPU:12 before, /device:TPU:97 now
where the time goes in v3:
time: 161 us
  Pallas kernels  158 us (98%)
  local copies, waits for them, and re-layouts  2.24 us (1%)
    pallas_call x1, Pallas kernels, shards(): pl.pallas_call(ladder_kernel, out_shape=jax.ShapeDtypeStruct((slabs, sub,...  158 us

profile of v3, /device:TPU:97, one launch (start us, length us, event | category | flops | bytes accessed | tf_op | source)
XLA Modules:
  0.0 160.7 jit_solution(9311084958929278656)
XLA Ops:
  0.0 158.5 %shard_map.46 = f32[2,64,1024]{2,1,0:T(8,128)} custom-call(f32[256,768]{1,0:T(8,128)} %a_ref.1, f32[12288,128]{1,0:T(8,128)} %bitcast.7, s32[8]{0:T(128)} %ab_ref.1, s32[2,8]{1,0:T(2,128)} %cd_ref.1), custom_call_target="tpu_custom_call" | custom-call | flops 19327352832 | bytes 8388608 | tf_op jit(solution)/shard_map/pallas_call | solution.py:402
  158.5 2.2 %copy.6 = f32[64,2,1024]{2,1,0:T(2,128)} copy(f32[64,2,1024]{2,0,1:T(8,128)} %bitcast.6) | data formatting | bytes 1048576 | tf_op jit(solution)/shard_map/transpose | solution.py:437

commit v4 on v3

--- a/solution.py
+++ b/solution.py
@@ -142,9 +142,9 @@
 
     def slot(k):
         far = (k == 5) | (k == 7)
-        near = (k == 3) | (k == 4)
-        r = jnp.where(k < 2, 0, jnp.where(far, 2, jnp.where(near, 1, 3)))
-        bit = jnp.where(near, 4 - k, lax.div(k, 4))
+        up = (k == 3) | (k == 6)
+        r = jnp.where(k < 2, 0, jnp.where(far, 2, jnp.where(up, 1, 3)))
+        bit = jnp.where(up, jnp.where(k == 3, 1, 0), lax.div(k, 4))
         bit = jnp.where(far, jnp.where(k == 7, zl, 1 - zl), bit)
         return r, jnp.where(k < 2, lax.rem(k + c, 2), bit)
 
@@ -322,6 +322,13 @@
 
         stages((3, finish))
 
+        stages(
+            (1, functools.partial(relay, 0)),
+            (4, functools.partial(relay, 1)),
+            (3, gather_side),
+            (5, collect),
+        )
+
         @pl.when(i == 1)
         def _():
             pass_on(1, 1)
@@ -346,13 +353,7 @@
             begin(11, 12)
             arrived(11, 12)
 
-        stages(
-            (-1, compute),
-            (1, functools.partial(relay, 0)),
-            (4, functools.partial(relay, 1)),
-            (3, gather_side),
-            (5, collect),
-        )
+        stages((-1, compute))
         return 0
 
     lax.fori_loop(0, 13, body, 0)

time: 161 us -> 159 us (0.988)
  the two profiles are of different devices: /device:TPU:97 before, /device:TPU:2 now
where the time goes in v4:
time: 159 us
  Pallas kernels  157 us (99%)
  local copies, waits for them, and re-layouts  2.24 us (1%)
    pallas_call x1, Pallas kernels, shards(): pl.pallas_call(ladder_kernel, out_shape=jax.ShapeDtypeStruct((slabs, sub,...  157 us

profile of v4, /device:TPU:2, one launch (start us, length us, event | category | flops | bytes accessed | tf_op | source)
XLA Modules:
  0.0 158.9 jit_solution(17802809079070384629)
XLA Ops:
  0.0 156.6 %shard_map.46 = f32[2,64,1024]{2,1,0:T(8,128)} custom-call(f32[256,768]{1,0:T(8,128)} %a_ref.1, f32[12288,128]{1,0:T(8,128)} %bitcast.7, s32[8]{0:T(128)} %ab_ref.1, s32[2,8]{1,0:T(2,128)} %cd_ref.1), custom_call_target="tpu_custom_call" | custom-call | flops 19327352832 | bytes 8388608 | tf_op jit(solution)/shard_map/pallas_call | solution.py:403
  156.6 2.2 %copy.6 = f32[64,2,1024]{2,1,0:T(2,128)} copy(f32[64,2,1024]{2,0,1:T(8,128)} %bitcast.6) | data formatting | bytes 1048576 | tf_op jit(solution)/shard_map/transpose | solution.py:438

commit v5 on v4

--- a/solution.py
+++ b/solution.py
@@ -13,7 +13,7 @@
 
 
 def ladder_kernel(
-    a_ref, b_hbm, ab_ref, cd_ref, out_ref,
+    a_ref, b_hbm, ab_ref, cd_ref, out_ref, acc,
     aall, ahl, braw, bh, bl, rowlab, py, px, yr, xp, xl, rp, rl, zr, zl2,
     b_sem, a_s, a_r, y_s, y_r, p_s, p_r, l_s, l_r, z_s, z_r,
 ):
@@ -359,13 +359,17 @@
     lax.fori_loop(0, 13, body, 0)
 
     k_own = slot_of(r_own, zl)
-    out_ref[:, :, :main] = py[:, k_own, mine, :]
-    out_ref[:, :, main:] = px[k_own, :, mine, :]
+    acc[:, :, :main] = py[:, k_own, mine, :]
+    acc[:, :, main:] = px[k_own, :, mine, :]
     for e in range(1, 8):
         spread(k_own, e // 4, e % 4).wait_recv()
-        out_ref[:, :, main:] += zl2[e]
+        acc[:, :, main:] += zl2[e]
     across(k_own).wait_recv()
-    out_ref[:, :, :main] += zr[...]
+    acc[:, :, :main] += zr[...]
+    for s in range(2):
+        for t in range(tiles):
+            lane = slice(t * LANES, (t + 1) * LANES)
+            out_ref[pl.ds(2 * t + s, sub, stride=2 * tiles), :] = acc[s, :, lane]
     across(k_own).wait_send()
     for e in range(1, 8):
         spread(k_own, e // 4, e % 4).wait_send()
@@ -402,10 +406,11 @@
     smem = pl.BlockSpec(memory_space=pltpu.SMEM)
     result = pl.pallas_call(
         ladder_kernel,
-        out_shape=jax.ShapeDtypeStruct((slabs, sub, cols), f32),
+        out_shape=jax.ShapeDtypeStruct((sub * tiles * slabs, LANES), f32),
         in_specs=[vmem, pl.BlockSpec(memory_space=pl.ANY), smem, smem],
         out_specs=vmem,
         scratch_shapes=[
+            pltpu.VMEM((slabs, sub, cols), f32),
             pltpu.VMEM((4, 2, rows, depth), f32),
             pltpu.VMEM((2 * rows, depth), bf16),
             pltpu.VMEM(flat.shape, f32),
@@ -435,7 +440,8 @@
             flops=6 * 8 * rows * depth * slabs * cols, bytes_accessed=8 * 2**20, transcendentals=0
         ),
     )(amplitudes, flat, ab_sizes, cd_sizes)
-    return jnp.transpose(result, (1, 0, 2))
+    result = jnp.transpose(result.reshape(sub, tiles, slabs, LANES), (0, 2, 1, 3))
+    return result.reshape(sub, slabs, cols)
 
 
 def solution(mesh):

time: 159 us -> 159 us (level)
    transpose x1 -> x0, local copies, waits for them, and re-layouts: 2.24 us -> none  [shards(): return jnp.transpose(result, (1, 0, 2))]
    unnamed x0 -> x1, local copies, waits for them, and re-layouts: none -> 1.87 us
where the time goes in v5:
time: 159 us
  Pallas kernels  157 us (99%)
  local copies, waits for them, and re-layouts  1.87 us (1%)
    pallas_call x1, Pallas kernels, shards(): pl.pallas_call(ladder_kernel, out_shape=jax.ShapeDtypeStruct((sub * tiles...  157 us

profile of v5, /device:TPU:2, one launch (start us, length us, event | category | flops | bytes accessed | tf_op | source)
XLA Modules:
  0.0 158.7 jit_solution(17795414029348157449)
XLA Ops:
  0.0 156.8 %shard_map.46 = f32[1024,128]{1,0:T(8,128)} custom-call(f32[256,768]{1,0:T(8,128)} %a_ref.1, f32[12288,128]{1,0:T(8,128)} %bitcast.11, s32[8]{0:T(128)} %ab_ref.1, s32[2,8]{1,0:T(2,128)} %cd_ref.1), custom_call_target="tpu_custom_call" | custom-call | flops 19327352832 | bytes 8388608 | tf_op jit(solution)/shard_map/pallas_call | solution.py:407
  156.8 1.9 %copy.8 = f32[64,2,1024]{2,1,0:T(2,128)} copy(f32[64,2,1024]{2,1,0:T(2,128)} %bitcast.10) | data formatting | bytes 1048576
